TPU v7x, 32 devices: a whole 2x2x4 slice. The times are simulated.
32 devices in a mesh: groups: 2 (over y), tiles: 8 (over z, x), section: 2 (over core).
Axes of the slice: x: 2, y: 2, z: 4, core: 2. Of those that a mesh axis runs over, the one named last changes fastest.
Arguments:
- object_slices: float32 [2, 2, 1024, 1024], P(None, 'section', ('groups', 'tiles')), parts along dimension 2
- probe_wave: float32 [2, 128, 128], replicated, may hold values from -4 to 4
- propagator: float32 [2, 128, 128], replicated
- tile_counts: int32 [16], P(('groups', 'tiles')), parts along dimension 0, may hold values from 0 to 12, as said below
- row_offsets: int32 [192], P(('groups', 'tiles')), parts along dimension 0, may hold values from 0 to 63
- column_offsets: int32 [192], P(('groups', 'tiles')), parts along dimension 0, may hold values from 0 to 896
- intensity: float32 [192, 128, 128], P(('groups', 'tiles')), parts along dimension 0, may hold values from 0 to 2
Outputs:
- object_grad: float32 [2, 2, 1024, 1024], P(None, 'section', ('groups', 'tiles')), parts along dimension 2
There are 2 independent parts, one for each index of `groups`. A program takes and returns all parts, laid end to end along the dimension named above; an argument that names none is the same for every part. Nothing has to cross between parts.
Inputs may be any that keep to these rules, and one draw needn't show every extreme that they name: Tile i owns the positions in its first tile_counts[i] slots; the last two tiles own none; all counts sum to 32; the positions of tiles 0 to i - 1 number at least 4 * i, and those of tiles 0 to i at most 4 * (i + 3).
All inputs are finite; a program needn't handle non-finite values.
Results may differ from a plain program's by a relative error of at most 0.014.
The roundings to bfloat16 on the way count: a program that leaves them out, or rounds other values in their place, can miss the bound.
Values may be sent and summed in bfloat16 or wider, within the bound.
A program may use at most 64 MiB of HBM per device.

v0:
```python
import math

import jax
import jax.numpy as jnp
from jax import lax
from jax.sharding import PartitionSpec as P


def shifted(value, axis, steps):
    count = lax.axis_size(axis)
    initial, last = (max(0, -steps), min(count, count - steps))
    return lax.ppermute(value, axis, [(source, source + steps) for source in range(initial, last)])


def fourier_table(wave_size):
    counter = jnp.arange(wave_size, dtype=jnp.int32)
    turned = counter[:, None] * counter[None, :] % wave_size
    angles = turned.astype(jnp.float32) * (2.0 * math.pi / wave_size)
    factor = 1.0 / math.sqrt(wave_size)
    return jnp.stack([jnp.cos(angles) * factor, -jnp.sin(angles) * factor])


def conjugate(matrix):
    return jnp.stack([matrix[0], -matrix[1]])


def complex_left(matrix, wavefield):
    products = jnp.einsum("cmn,bdnk->bcdmk", matrix, wavefield, preferred_element_type=jnp.float32)
    return jnp.stack(
        [products[:, 0, 0] - products[:, 1, 1], products[:, 0, 1] + products[:, 1, 0]], axis=1
    )


def complex_right(wavefield, matrix):
    products = jnp.einsum("bdmn,cnk->bdcmk", wavefield, matrix, preferred_element_type=jnp.float32)
    return jnp.stack(
        [products[:, 0, 0] - products[:, 1, 1], products[:, 0, 1] + products[:, 1, 0]], axis=1
    )


def sandwich(matrix, wavefield):
    halfway = complex_left(matrix, wavefield).astype(jnp.bfloat16)
    return complex_right(halfway, matrix)


def complex_times(left_side, right_side):
    return jnp.stack(
        [
            left_side[:, 0] * right_side[:, 0] - left_side[:, 1] * right_side[:, 1],
            left_side[:, 0] * right_side[:, 1] + left_side[:, 1] * right_side[:, 0],
        ],
        axis=1,
    )


def conjugate_times(left_side, right_side):
    return jnp.stack(
        [
            left_side[:, 0] * right_side[:, 0] + left_side[:, 1] * right_side[:, 1],
            left_side[:, 0] * right_side[:, 1] - left_side[:, 1] * right_side[:, 0],
        ],
        axis=1,
    )


def forward_slices(wavefield, patches, propagator_b):
    saved_waves = [wavefield]
    product = complex_times(wavefield.astype(jnp.float32), patches[:, :, 0]).astype(jnp.bfloat16)
    wavefield = sandwich(propagator_b, product).astype(jnp.bfloat16)
    return (wavefield, jnp.stack(saved_waves, axis=2))


def far_field(wavefield, measured, live_slots, fourier_b):
    far_wave = sandwich(fourier_b, wavefield)
    excess = far_wave[:, 0] * far_wave[:, 0] + far_wave[:, 1] * far_wave[:, 1] - measured
    misfit = (far_wave * (excess * live_slots[:, None, None])[:, None]).astype(jnp.bfloat16)
    return sandwich(conjugate(fourier_b), misfit).astype(jnp.bfloat16)


def backward_slices(adjoint, patches, saved_waves, propagator_conj):
    gradients = [None] * patches.shape[2]
    for layer_index in reversed(range(patches.shape[2])):
        backward = sandwich(propagator_conj, adjoint)
        gradients[layer_index] = conjugate_times(
            saved_waves[:, :, layer_index].astype(jnp.float32), backward
        )
        adjoint = conjugate_times(patches[:, :, layer_index], backward).astype(jnp.bfloat16)
    return (adjoint, jnp.stack(gradients, axis=2))


def extract(source, starts, columns, wave_size):

    def take_window(start_row, column):
        return lax.dynamic_slice(
            source,
            (0, 0, start_row, column),
            (source.shape[0], source.shape[1], wave_size, wave_size),
        )

    return jax.vmap(take_window)(starts, columns)


def deposit(summed, gradients, starts, columns):

    def add_one(slot_index, summed):
        corner = (0, 0, starts[slot_index], columns[slot_index])
        patch_grad = gradients[slot_index]
        current = lax.dynamic_slice(summed, corner, patch_grad.shape)
        return lax.dynamic_update_slice(summed, current + patch_grad, corner)

    return lax.fori_loop(0, gradients.shape[0], add_one, summed)


def shards(
    object_slices, probe_wave, propagator, tile_counts, row_offsets, column_offsets, intensity
):
    wave_size = probe_wave.shape[1]
    tile_rows = object_slices.shape[2]
    slot_total = row_offsets.shape[0]
    section_count = lax.axis_size("section")
    section_id = lax.axis_index("section")
    fourier_b = fourier_table(wave_size).astype(jnp.bfloat16)
    propagator_b = propagator.astype(jnp.bfloat16)
    propagator_conj = conjugate(propagator_b)
    live_slots = (jnp.arange(slot_total, dtype=jnp.int32) < tile_counts[0]).astype(jnp.float32)
    row_bands = [object_slices]
    for shift_by in (-1, -2):
        row_bands.append(shifted(object_slices, "tiles", shift_by))
    extended = jnp.concatenate(row_bands, axis=2)
    start_wave = probe_wave.astype(jnp.bfloat16)
    block_count = slot_total // slot_total
    tick_count = block_count + section_count - 1
    all_patches = extract(extended, row_offsets, column_offsets, wave_size)
    is_first = section_id == 0
    is_last = section_id == section_count - 1
    blank = jnp.zeros((slot_total, 2, wave_size, wave_size), jnp.bfloat16)
    start_group = jnp.broadcast_to(start_wave[None], blank.shape)
    saved_all = jnp.zeros(all_patches.shape, jnp.bfloat16)
    adjoint_all = jnp.zeros((slot_total, 2, wave_size, wave_size), jnp.bfloat16)
    carried = blank
    for tick_step in range(tick_count):
        block_index = tick_step - section_id
        active = (block_index >= 0) & (block_index < block_count)
        first_slot = jnp.clip(block_index, 0, block_count - 1) * slot_total

        def run_forward(stored):
            saved_all, adjoint_all = stored
            incoming = jnp.where(is_first, start_group, carried)
            outgoing, saved_waves = forward_slices(incoming, all_patches, propagator_b)
            saved_all = lax.dynamic_update_slice_in_dim(saved_all, saved_waves, first_slot, 0)

            def finish(exit_wave):
                return far_field(exit_wave, intensity, live_slots, fourier_b)

            adjoint = lax.cond(is_last, finish, lambda unchanged: unchanged, outgoing)
            adjoint_all = adjoint
            return ((saved_all, adjoint_all), outgoing)

        def skip_forward(stored):
            return (stored, blank)

        (saved_all, adjoint_all), outgoing = lax.cond(
            active, run_forward, skip_forward, (saved_all, adjoint_all)
        )
        if tick_step + 1 < tick_count:
            carried = shifted(outgoing, "section", 1)
    summed = jnp.zeros(extended.shape, jnp.float32)
    carried = blank
    for tick_step in range(tick_count):
        block_index = tick_step - (section_count - 1 - section_id)
        active = (block_index >= 0) & (block_index < block_count)
        first_slot = jnp.clip(block_index, 0, block_count - 1) * slot_total

        def run_backward(summed):
            incoming = jnp.where(is_last, adjoint_all, carried)
            outgoing, gradients = backward_slices(incoming, all_patches, saved_all, propagator_conj)
            summed = deposit(summed, gradients, row_offsets, column_offsets)
            return (summed, outgoing)

        def skip_backward(summed):
            return (summed, blank)

        summed, outgoing = lax.cond(active, run_backward, skip_backward, summed)
        if tick_step + 1 < tick_count:
            carried = shifted(outgoing, "section", -1)
    result = summed[:, :, :tile_rows]
    for shift_by in (1, 2):
        result = result + shifted(
            summed[:, :, shift_by * tile_rows : (shift_by + 1) * tile_rows], "tiles", shift_by
        )
    return result


def solution(mesh):
    placed = (
        P(None, "section", ("groups", "tiles"), None),
        P(),
        P(),
        P(("groups", "tiles")),
        P(("groups", "tiles")),
        P(("groups", "tiles")),
        P(("groups", "tiles"), None, None),
    )
    return jax.shard_map(
        shards,
        mesh=mesh,
        in_specs=placed,
        out_specs=P(None, "section", ("groups", "tiles"), None),
        check_vma=False,
    )
```

profile of v0, /device:TPU:10, one launch (start us, length us, event | category | flops | bytes accessed | tf_op | source)
XLA Modules:
  0.0 342.8 jit_solution(16216050799434690161)
XLA Ops:
  0.0 2.4 collective-permute-start
  2.4 1.9 collective-permute-start.1
  8.1 9.7 %collective-permute-done = f32[2,1,64,1024]{3,2,1,0:T(8,128)S(1)} collective-permute-done((f32[2,1,64,1024]{3,2,1,0:T(8,128)}, f32[2,1,64,1024]{3,2,1,0:T(8,128)S(1)}, u32[]{:S(2)}, u32[]{:S(2)}) %collective-permute-start) | collective-permute-done | bytes 524320 | tf_op jit(solution)/shard_map/ppermute | solution.py:12
  18.6 1.5 pad_maximum_fusion.11
  20.1 23.0 %while.27 = (s32[]{:T(128)}, f32[2,1,192,1024]{3,2,1,0:T(8,128)S(1)}, s32[12,4]{0,1:T(4,128)S(1)}, f32[12,2,1,128,128]{4,3,1,2,0:T(8,128)S(1)}, s32[]{:T(128)}) while((s32[]{:T(128)}, f32[2,1,192,1024]{3,2,1,0:T(8,128)S(1)}, s32[12,4]{0,1:T(4,128)S(1)}, f32[12,2,1,128,128]{4,3,1,2,0:T(8,128)S(1)}, s32[]{:T(128)}) %tuple.151), condition=%wide.while_cond, body=%wide.while_body.sunk | while | flops 2 | bytes 262269 | solution.py:94
  20.7 1.3 bitcast_dynamic-update-slice_fusion.2
  22.6 1.3 bitcast_dynamic-update-slice_fusion.2
  24.5 1.3 bitcast_dynamic-update-slice_fusion.2
  26.4 1.3 bitcast_dynamic-update-slice_fusion.2
  28.3 1.3 bitcast_dynamic-update-slice_fusion.2
  30.2 1.3 bitcast_dynamic-update-slice_fusion.2
  32.2 1.3 bitcast_dynamic-update-slice_fusion.2
  34.1 1.3 bitcast_dynamic-update-slice_fusion.2
  36.0 1.3 bitcast_dynamic-update-slice_fusion.2
  37.9 1.3 bitcast_dynamic-update-slice_fusion.2
  43.2 10.4 %conditional.6 = (bf16[12,2,1,128,128]{3,4,1,0,2:T(8,128)(2,1)}, bf16[12,2,128,128]{2,3,0,1:T(8,128)(2,1)}, bf16[12,2,128,128]{3,2,0,1:T(8,128)(2,1)}) conditional(s32[]{:T(128)} %convert_element_type.100, () %tuple.81, (pred[]{:T(512)}, bf16[12,2,128,128]{2,3,1,0:T(8,128)(2,1)S(1)}, pred[]{:T(512)}, f32[12,2,1,128,128]{4,3,1,2,0:T(8,128)S(1)}, ...), branch_computations={%region_0.1_spmd, %region_1.4_spmd} | conditional | flops 1221017600 | bytes 71303320 | solution.py:162
  43.2 1.6 fusion.39
  44.9 1.6 copy.56
  46.5 2.1 subtract_convert_fusion
  51.3 2.3 conditional
  51.3 2.3 copy.119
  53.6 1.5 copy.57
  55.1 2.2 collective-permute-start.2
  59.1 2.4 conditional.8
  59.1 1.4 broadcast_in_dim.2
  61.6 1.5 copy.62
  64.4 129.8 %collective-permute-done.3 = bf16[12,2,128,128]{2,3,1,0:T(8,128)(2,1)S(1)} collective-permute-done((bf16[12,2,128,128]{2,3,1,0:T(8,128)(2,1)S(1)}, bf16[12,2,128,128]{2,3,1,0:T(8,128)(2,1)S(1)}, u32[]{:S(2)}, u32[]{:S(2)}) %collective-permute-start.3) | collective-permute-done | bytes 786464 | tf_op jit(solution)/shard_map/ppermute | solution.py:12
  194.2 119.8 %conditional.9 = (f32[2,1,192,1024]{3,2,1,0:T(8,128)}) conditional(s32[]{:T(128)} %convert_element_type.97, f32[2,1,192,1024]{3,2,1,0:T(8,128)} %get-tuple-element.380, (bf16[12,2,1,128,128]{3,4,1,0,2:T(8,128)(2,1)}, pred[]{:T(512)}, bf16[12,2,128,128]{2,3,0,1:T(8,128)(2,1)}, bf16[12,2,128,128]{2,3,1,0:T(8,128)(2,1)S(1)}, ...), branch_computations={%region_12.13_spmd, %region_13.16_spmd} | conditional | flops 406618112 | bytes 26738976 | solution.py:183
  194.2 1.7 convolution_bitcast_fusion.15
  196.6 2.3 copy.63
  200.8 113.2 %while.25 = (s32[]{:T(128)}, f32[2,1,192,1024]{3,2,1,0:T(8,128)}, s32[12]{0:T(128)S(1)}, s32[12]{0:T(128)S(1)}, f32[12,2,1,128,128]{4,3,0,1,2:T(8,128)S(1)}, /*index=5*/s32[]{:T(128)}, s32[]{:T(128)}, s32[]{:T(128)}, s32[]{:T(128)}) while((s32[]{:T(128)}, f32[2,1,192,1024]{3,2,1,0:T(8,128)}, s32[12]{0:T(128)S(1)}, s32[12]{0:T(128)S(1)}, ...), condition=%wide.region_15.15_spmd, body=%wide.region_14.14_spmd.sunk | while | flops 32776 | bytes 655561 | solution.py:111
  206.8 3.5 %dynamic_update_slice.18 = f32[2,1,192,1024]{3,2,1,0:T(8,128)} dynamic-update-slice(f32[2,1,192,1024]{3,2,1,0:T(8,128)} %get-tuple-element.610, f32[2,1,128,128]{3,2,1,0:T(8,128)S(1)} %bitcast_add_fusion.4, s32[]{:T(128)} %constant.114.clone..sunk, s32[]{:T(128)} %constant.114.clone..sunk, s32[]{:T(128)S(6)} %select_n.162, s32[]{:T(128)S(6)} %select_n.163) | dynamic-update-slice | bytes 262148 | tf_op jit(solution)/shard_map/cond/branch_1_fun/while/body/eval_jaxpr/dynamic_update_slice | solution.py:109
  216.2 3.4 dynamic_update_slice.18
  225.6 3.4 dynamic_update_slice.18
  234.9 3.5 %dynamic_update_slice.18 = f32[2,1,192,1024]{3,2,1,0:T(8,128)} dynamic-update-slice(f32[2,1,192,1024]{3,2,1,0:T(8,128)} %get-tuple-element.610, f32[2,1,128,128]{3,2,1,0:T(8,128)S(1)} %bitcast_add_fusion.4, s32[]{:T(128)} %constant.114.clone..sunk, s32[]{:T(128)} %constant.114.clone..sunk, s32[]{:T(128)S(6)} %select_n.162, s32[]{:T(128)S(6)} %select_n.163) | dynamic-update-slice | bytes 262148 | tf_op jit(solution)/shard_map/cond/branch_1_fun/while/body/eval_jaxpr/dynamic_update_slice | solution.py:109
  244.4 3.6 %dynamic_update_slice.18 = f32[2,1,192,1024]{3,2,1,0:T(8,128)} dynamic-update-slice(f32[2,1,192,1024]{3,2,1,0:T(8,128)} %get-tuple-element.610, f32[2,1,128,128]{3,2,1,0:T(8,128)S(1)} %bitcast_add_fusion.4, s32[]{:T(128)} %constant.114.clone..sunk, s32[]{:T(128)} %constant.114.clone..sunk, s32[]{:T(128)S(6)} %select_n.162, s32[]{:T(128)S(6)} %select_n.163) | dynamic-update-slice | bytes 262148 | tf_op jit(solution)/shard_map/cond/branch_1_fun/while/body/eval_jaxpr/dynamic_update_slice | solution.py:109
  253.9 3.5 %dynamic_update_slice.18 = f32[2,1,192,1024]{3,2,1,0:T(8,128)} dynamic-update-slice(f32[2,1,192,1024]{3,2,1,0:T(8,128)} %get-tuple-element.610, f32[2,1,128,128]{3,2,1,0:T(8,128)S(1)} %bitcast_add_fusion.4, s32[]{:T(128)} %constant.114.clone..sunk, s32[]{:T(128)} %constant.114.clone..sunk, s32[]{:T(128)S(6)} %select_n.162, s32[]{:T(128)S(6)} %select_n.163) | dynamic-update-slice | bytes 262148 | tf_op jit(solution)/shard_map/cond/branch_1_fun/while/body/eval_jaxpr/dynamic_update_slice | solution.py:109
  263.3 3.4 dynamic_update_slice.18
  272.6 3.5 %dynamic_update_slice.18 = f32[2,1,192,1024]{3,2,1,0:T(8,128)} dynamic-update-slice(f32[2,1,192,1024]{3,2,1,0:T(8,128)} %get-tuple-element.610, f32[2,1,128,128]{3,2,1,0:T(8,128)S(1)} %bitcast_add_fusion.4, s32[]{:T(128)} %constant.114.clone..sunk, s32[]{:T(128)} %constant.114.clone..sunk, s32[]{:T(128)S(6)} %select_n.162, s32[]{:T(128)S(6)} %select_n.163) | dynamic-update-slice | bytes 262148 | tf_op jit(solution)/shard_map/cond/branch_1_fun/while/body/eval_jaxpr/dynamic_update_slice | solution.py:109
  282.0 3.4 %dynamic_update_slice.18 = f32[2,1,192,1024]{3,2,1,0:T(8,128)} dynamic-update-slice(f32[2,1,192,1024]{3,2,1,0:T(8,128)} %get-tuple-element.610, f32[2,1,128,128]{3,2,1,0:T(8,128)S(1)} %bitcast_add_fusion.4, s32[]{:T(128)} %constant.114.clone..sunk, s32[]{:T(128)} %constant.114.clone..sunk, s32[]{:T(128)S(6)} %select_n.162, s32[]{:T(128)S(6)} %select_n.163) | dynamic-update-slice | bytes 262148 | tf_op jit(solution)/shard_map/cond/branch_1_fun/while/body/eval_jaxpr/dynamic_update_slice | solution.py:109
  291.4 3.5 %dynamic_update_slice.18 = f32[2,1,192,1024]{3,2,1,0:T(8,128)} dynamic-update-slice(f32[2,1,192,1024]{3,2,1,0:T(8,128)} %get-tuple-element.610, f32[2,1,128,128]{3,2,1,0:T(8,128)S(1)} %bitcast_add_fusion.4, s32[]{:T(128)} %constant.114.clone..sunk, s32[]{:T(128)} %constant.114.clone..sunk, s32[]{:T(128)S(6)} %select_n.162, s32[]{:T(128)S(6)} %select_n.163) | dynamic-update-slice | bytes 262148 | tf_op jit(solution)/shard_map/cond/branch_1_fun/while/body/eval_jaxpr/dynamic_update_slice | solution.py:109
  300.9 3.5 %dynamic_update_slice.18 = f32[2,1,192,1024]{3,2,1,0:T(8,128)} dynamic-update-slice(f32[2,1,192,1024]{3,2,1,0:T(8,128)} %get-tuple-element.610, f32[2,1,128,128]{3,2,1,0:T(8,128)S(1)} %bitcast_add_fusion.4, s32[]{:T(128)} %constant.114.clone..sunk, s32[]{:T(128)} %constant.114.clone..sunk, s32[]{:T(128)S(6)} %select_n.162, s32[]{:T(128)S(6)} %select_n.163) | dynamic-update-slice | bytes 262148 | tf_op jit(solution)/shard_map/cond/branch_1_fun/while/body/eval_jaxpr/dynamic_update_slice | solution.py:109
  310.4 3.6 %dynamic_update_slice.18 = f32[2,1,192,1024]{3,2,1,0:T(8,128)} dynamic-update-slice(f32[2,1,192,1024]{3,2,1,0:T(8,128)} %get-tuple-element.610, f32[2,1,128,128]{3,2,1,0:T(8,128)S(1)} %bitcast_add_fusion.4, s32[]{:T(128)} %constant.114.clone..sunk, s32[]{:T(128)} %constant.114.clone..sunk, s32[]{:T(128)S(6)} %select_n.162, s32[]{:T(128)S(6)} %select_n.163) | dynamic-update-slice | bytes 262148 | tf_op jit(solution)/shard_map/cond/branch_1_fun/while/body/eval_jaxpr/dynamic_update_slice | solution.py:109
  315.3 10.7 %collective-permute-start.4 = (f32[2,1,64,1024]{3,2,1,0:T(8,128)S(1)}, f32[2,1,64,1024]{3,2,1,0:T(8,128)S(1)}, u32[]{:S(2)}, u32[]{:S(2)}) collective-permute-start(f32[2,1,64,1024]{3,2,1,0:T(8,128)S(1)} %get-tuple-element.501), channel_id=1, source_target_pairs={{0,2},{2,4},{4,6},{6,8},{8,10},{10,12},{12,14},{1,3},{3,5},{5,7},{... | collective-permute-start | bytes 1572872 | tf_op jit(solution)/shard_map/ppermute | solution.py:12
  326.0 2.7 collective-permute-start.5
  328.8 5.0 %collective-permute-done.4 = f32[2,1,64,1024]{3,2,1,0:T(8,128)S(1)} collective-permute-done((f32[2,1,64,1024]{3,2,1,0:T(8,128)S(1)}, f32[2,1,64,1024]{3,2,1,0:T(8,128)S(1)}, u32[]{:S(2)}, u32[]{:S(2)}) %collective-permute-start.4) | collective-permute-done | bytes 524320 | tf_op jit(solution)/shard_map/ppermute | solution.py:12
  333.8 7.1 %collective-permute-done.5 = f32[2,1,64,1024]{3,2,1,0:T(8,128)S(1)} collective-permute-done((f32[2,1,64,1024]{3,2,1,0:T(8,128)S(1)}, f32[2,1,64,1024]{3,2,1,0:T(8,128)S(1)}, u32[]{:S(2)}, u32[]{:S(2)}) %collective-permute-start.5) | collective-permute-done | bytes 524320 | tf_op jit(solution)/shard_map/ppermute | solution.py:12
  340.9 1.9 fusion.124
  (103 shorter events, 52.0 us)
Async XLA Ops:
  0.0 17.8 %collective-permute-start = (f32[2,1,64,1024]{3,2,1,0:T(8,128)}, f32[2,1,64,1024]{3,2,1,0:T(8,128)S(1)}, u32[]{:S(2)}, u32[]{:S(2)}) collective-permute-start(f32[2,1,64,1024]{3,2,1,0:T(8,128)} %param.23), channel_id=1, source_target_pairs={{2,0},{4,2},{6,4},{8,6},{10,8},{12,10},{14,12},{3,1},{5,3},{7,5},{... | collective-permute-start | bytes 1572872 | tf_op jit(solution)/shard_map/ppermute | solution.py:12
  2.4 16.2 %collective-permute-start.1 = (f32[2,1,64,1024]{3,2,1,0:T(8,128)}, f32[2,1,64,1024]{3,2,1,0:T(8,128)}, u32[]{:S(2)}, u32[]{:S(2)}) collective-permute-start(f32[2,1,64,1024]{3,2,1,0:T(8,128)} %param.23), channel_id=1, source_target_pairs={{4,0},{6,2},{8,4},{10,6},{12,8},{14,10},{5,1},{7,3},{9,5},{11,7},{... | collective-permute-start | bytes 1572872 | tf_op jit(solution)/shard_map/ppermute | solution.py:12
  17.8 0.8 copy-start.4
  50.1 1.3 copy-start
  55.1 3.3 collective-permute-start.2
  58.4 0.7 copy-start.5
  58.5 0.7 copy-start.6
  63.1 131.1 %collective-permute-start.3 = (bf16[12,2,128,128]{2,3,1,0:T(8,128)(2,1)S(1)}, bf16[12,2,128,128]{2,3,1,0:T(8,128)(2,1)S(1)}, u32[]{:S(2)}, u32[]{:S(2)}) collective-permute-start(bf16[12,2,128,128]{2,3,1,0:T(8,128)(2,1)S(1)} %copy.62), channel_id=1, source_target_pairs={{1,0},{3,2},{5,4},{7,6},{9,8},{11,10},{13,12},{15,14},{17,16},{19,... | collective-permute-start | bytes 2359304 | tf_op jit(solution)/shard_map/ppermute | solution.py:12
  315.3 18.5 %collective-permute-start.4 = (f32[2,1,64,1024]{3,2,1,0:T(8,128)S(1)}, f32[2,1,64,1024]{3,2,1,0:T(8,128)S(1)}, u32[]{:S(2)}, u32[]{:S(2)}) collective-permute-start(f32[2,1,64,1024]{3,2,1,0:T(8,128)S(1)} %get-tuple-element.501), channel_id=1, source_target_pairs={{0,2},{2,4},{4,6},{6,8},{8,10},{10,12},{12,14},{1,3},{3,5},{5,7},{... | collective-permute-start | bytes 1572872 | tf_op jit(solution)/shard_map/ppermute | solution.py:12
  326.0 14.8 %collective-permute-start.5 = (f32[2,1,64,1024]{3,2,1,0:T(8,128)S(1)}, f32[2,1,64,1024]{3,2,1,0:T(8,128)S(1)}, u32[]{:S(2)}, u32[]{:S(2)}) collective-permute-start(f32[2,1,64,1024]{3,2,1,0:T(8,128)S(1)} %get-tuple-element.502), channel_id=1, source_target_pairs={{0,4},{2,6},{4,8},{6,10},{8,12},{10,14},{1,5},{3,7},{5,9},{7,11},{... | collective-permute-start | bytes 1572872 | tf_op jit(solution)/shard_map/ppermute | solution.py:12
where the time goes:
time: 348 us; the launch traced here: 343 us
  waiting for transfers between devices  153 us (44%)
  local copies, waits for them, and re-layouts  94.1 us (27%)
  loops' own time  44.1 us (13%)
  other arithmetic  26.3 us (8%)
  starting transfers between devices  21.3 us (6%)
    ppermute x6, waiting for transfers between devices, shifted(): lax.ppermute(value, axis, [(source, source + steps) for source in range(i...  153 us
    another operation x1, loops' own time, deposit(): return lax.fori_loop(0, gradients.shape[0], add_one, summed)  43.7 us
    dynamic_update_slice x12, local copies, waits for them, and re-layouts, add_one(): return lax.dynamic_update_slice(summed, current + patch_grad, corner)  41.8 us
    gather x36, local copies, waits for them, and re-layouts  22.7 us
    ppermute x6, starting transfers between devices, shifted(): lax.ppermute(value, axis, [(source, source + steps) for source in range(i...  21.3 us
    dynamic_slice x24, local copies, waits for them, and re-layouts, add_one(): corner = (0, 0, starts[slot_index], columns[slot_index])  14.7 us
    add x12, other arithmetic, add_one(): return lax.dynamic_update_slice(summed, current + patch_grad, corner)  13 us
  transfers between devices with their start and end apart: 6, of which 5 were waited for; matrix products, arithmetic and copies ran while one was open for 1% of the time, Pallas kernels for 0%

commit v1 on v0

v1 whole, which is shorter than its diff:
```python
import math

import jax
import jax.numpy as jnp
import numpy as np
from jax import lax
from jax.experimental import pallas as pl
from jax.experimental.pallas import tpu as pltpu
from jax.sharding import PartitionSpec as P

MESH = pl.DeviceIdType.MESH
BF16 = jnp.bfloat16
F32 = jnp.float32


def fourier_blocks(wave_size):
    counter = np.arange(wave_size)
    turned = (counter[:, None] * counter[None, :] % wave_size).astype(np.float32)
    angles = turned * np.float32(2.0 * math.pi / wave_size)
    factor = np.float32(1.0 / math.sqrt(wave_size))
    real = (np.cos(angles) * factor).astype(np.float32)
    imag = (-np.sin(angles) * factor).astype(np.float32)
    plain = np.block([[real, imag], [-imag, real]])
    turned = np.block([[real, -imag], [imag, real]])
    return jnp.asarray(np.stack([plain, turned]).astype(jnp.bfloat16))


def dot(left_side, right_side):
    return jnp.dot(left_side, right_side, preferred_element_type=F32)


def sandwich(left_block, right_block, waves):
    size = waves[0][0].shape[0]
    stacked = jnp.concatenate([jnp.concatenate([real, imag], axis=0) for real, imag in waves], axis=1)
    halfway = dot(left_block, stacked).astype(BF16)
    results = []
    for p in range(len(waves)):
        columns = slice(p * size, (p + 1) * size)
        row = jnp.concatenate([halfway[:size, columns], halfway[size:, columns]], axis=1)
        full = dot(row, right_block)
        results.append((full[:, :size], full[:, size:]))
    return results


def times(a, b):
    return (a[0] * b[0] - a[1] * b[1], a[0] * b[1] + a[1] * b[0])


def conj_times(a, b):
    return (a[0] * b[0] + a[1] * b[1], a[0] * b[1] - a[1] * b[0])


def cast(pair, dtype):
    return (pair[0].astype(dtype), pair[1].astype(dtype))


def kernel(
    tile_count, counts, row_offsets, column_offsets, object_ref, probe_ref, propagator_ref,
    fourier_ref, intensity_hbm, out_ref, bands, strips, pick, place, pick_rows, place_rows, partial, to_partner,
    from_partner, to_tiles, from_tiles, measured, send_sem, recv_sem, load_sem,
):
    size = probe_ref.shape[1]
    rows = object_ref.shape[2]
    width = object_ref.shape[3]
    mine = measured.shape[0]
    tile = lax.axis_index("tiles")
    core = lax.axis_index("section")
    other = 1 - core
    first = core * mine

    load = pltpu.make_async_copy(intensity_hbm.at[pl.ds(first, mine)], measured, load_sem)
    load.start()

    def remote(src, dst, index, where):
        return pltpu.make_async_remote_copy(
            src_ref=src, dst_ref=dst, send_sem=send_sem.at[index], recv_sem=recv_sem.at[index],
            device_id=where, device_id_type=MESH,
        )

    partner = {"section": other}

    def towards(step):
        return {"tiles": tile + step}

    barrier = pltpu.get_barrier_semaphore()
    pl.semaphore_signal(barrier, inc=1, device_id=partner, device_id_type=MESH)
    arrivals = jnp.int32(1)
    for step in (-2, -1, 1, 2):
        there = (tile + step >= 0) & (tile + step < tile_count)
        arrivals = arrivals + there.astype(jnp.int32)

        @pl.when(there)
        def _():
            pl.semaphore_signal(barrier, inc=1, device_id=towards(step), device_id_type=MESH)

    for plane in range(2):
        bands[core, 0, plane * rows : (plane + 1) * rows, :] = object_ref[plane, 0].astype(BF16)
    pl.semaphore_wait(barrier, arrivals)

    own = remote(bands.at[core, 0], bands.at[core, 0], 0, partner)
    for ahead in (1, 2):

        @pl.when(tile >= ahead)
        def _():
            remote(bands.at[core, 0], bands.at[core, ahead], ahead, towards(-ahead)).start()

    own.start()

    spots = lax.broadcasted_iota(jnp.int32, (size, width), 1)
    counter = lax.broadcasted_iota(jnp.int32, (size, width), 0)
    down_spots = lax.broadcasted_iota(jnp.int32, (width, size), 0)
    down_counter = lax.broadcasted_iota(jnp.int32, (width, size), 1)
    row_spots = lax.broadcasted_iota(jnp.int32, (size, 3 * rows), 1)
    row_counter = lax.broadcasted_iota(jnp.int32, (size, 3 * rows), 0)
    down_row_spots = lax.broadcasted_iota(jnp.int32, (3 * rows, size), 0)
    down_row_counter = lax.broadcasted_iota(jnp.int32, (3 * rows, size), 1)
    for p in range(mine):
        column = column_offsets[first + p]
        offset = row_offsets[first + p]
        pick[:, p * size : (p + 1) * size] = jnp.where(down_spots == down_counter + column, 1.0, 0.0).astype(BF16)
        place[p * size : (p + 1) * size, :] = jnp.where(spots == counter + column, 1.0, 0.0).astype(BF16)
        pick_rows[p] = jnp.where(row_spots == row_counter + offset, 1.0, 0.0).astype(BF16)
        place_rows[p] = jnp.where(down_row_spots == down_row_counter + offset, 1.0, 0.0).astype(BF16)
    prop = (propagator_ref[0].astype(BF16), propagator_ref[1].astype(BF16))

    def block(a, b, c, d):
        return jnp.concatenate([jnp.concatenate([a, b], axis=1), jnp.concatenate([c, d], axis=1)], axis=0)

    prop_plain = block(prop[0], prop[1], -prop[1], prop[0])
    prop_turned = block(prop[0], -prop[1], prop[1], prop[0])
    four_plain = fourier_ref[0]
    four_turned = fourier_ref[1]

    def extract(layer, b):
        found = dot(bands[layer, b], pick[...]).astype(BF16)
        for p in range(mine):
            for plane in range(2):
                strips[layer, p, b * rows : (b + 1) * rows, plane * size : (plane + 1) * size] = found[
                    plane * rows : (plane + 1) * rows, p * size : (p + 1) * size
                ]

    for ahead in (1, 2):

        @pl.when(tile + ahead >= tile_count)
        def _():
            for layer in range(2):
                bands[layer, ahead] = jnp.zeros((2 * rows, width), BF16)

    extract(core, 0)
    own.wait()
    extract(other, 0)
    for ahead in (1, 2):

        @pl.when(tile + ahead < tile_count)
        def _():
            here = bands.at[core, ahead]
            remote(here, here, ahead, partner).wait_recv()
            remote(here, here, 2 + ahead, partner).start()

        extract(core, ahead)

    for ahead in (1, 2):

        @pl.when(tile + ahead < tile_count)
        def _():
            here = bands.at[core, ahead]
            there = bands.at[other, ahead]
            remote(there, there, 2 + ahead, partner).wait_recv()
            remote(here, here, 2 + ahead, partner).wait_send()

        @pl.when(tile >= ahead)
        def _():
            remote(bands.at[core, 0], bands.at[core, ahead], ahead, towards(-ahead)).wait_send()

        extract(other, ahead)

    patches = [[None] * mine for _ in range(2)]
    for layer in range(2):
        for p in range(mine):
            found = dot(pick_rows[p], strips[layer, p])
            patches[layer][p] = (found[:, :size], found[:, size:])

    start = (probe_ref[0].astype(BF16).astype(F32), probe_ref[1].astype(BF16).astype(F32))
    product = [cast(times(start, patches[0][p]), BF16) for p in range(mine)]
    middle = [cast(z, BF16) for z in sandwich(prop_turned, prop_plain, product)]
    product = [cast(times(cast(middle[p], F32), patches[1][p]), BF16) for p in range(mine)]
    exit_waves = [cast(z, BF16) for z in sandwich(prop_turned, prop_plain, product)]
    far = sandwich(four_turned, four_plain, exit_waves)
    load.wait()
    misfit = []
    for p in range(mine):
        real, imag = far[p]
        excess = real * real + imag * imag - measured[p]
        live = jnp.full((size, size), first + p, jnp.int32) < counts[0]
        misfit.append(
            (jnp.where(live, excess * real, 0.0).astype(BF16), jnp.where(live, excess * imag, 0.0).astype(BF16))
        )
    adjoint = [cast(z, BF16) for z in sandwich(four_plain, four_turned, misfit)]

    def deposit(layer, gradients):
        shifted = [
            dot(place_rows[p], jnp.concatenate(cast(gradients[p], BF16), axis=1)).astype(BF16) for p in range(mine)
        ]
        for b in (1, 2, 0):
            pieces = [
                jnp.concatenate(
                    [s[b * rows : (b + 1) * rows, plane * size : (plane + 1) * size] for s in shifted], axis=1
                )
                for plane in range(2)
            ]
            partial[layer, b] = dot(jnp.concatenate(pieces, axis=0), place[...])

    back = sandwich(prop_plain, prop_turned, adjoint)
    deposit(1, [conj_times(cast(middle[p], F32), back[p]) for p in range(mine)])
    adjoint = [cast(conj_times(patches[1][p], back[p]), BF16) for p in range(mine)]
    back = sandwich(prop_plain, prop_turned, adjoint)
    deposit(0, [conj_times(start, back[p]) for p in range(mine)])

    swaps = []
    for b in (1, 2, 0):
        to_partner[b] = partial[other, b].astype(BF16)
        swap = remote(to_partner.at[b], from_partner.at[b], 5 + b, partner)
        swap.start()
        swaps.append(swap)
    for b, swap in zip((1, 2), swaps):
        swap.wait()
        to_tiles[b - 1] = (partial[core, b] + from_partner[b].astype(F32)).astype(BF16)

        @pl.when(tile + b < tile_count)
        def _():
            remote(to_tiles.at[b - 1], from_tiles.at[b - 1], 7 + b, towards(b)).start()

    swaps[2].wait()
    total = partial[core, 0] + from_partner[0].astype(F32)
    for plane in range(2):
        out_ref[plane, 0] = total[plane * rows : (plane + 1) * rows]
    for b in (1, 2):

        @pl.when(tile >= b)
        def _():
            remote(to_tiles.at[b - 1], from_tiles.at[b - 1], 7 + b, partner).wait_recv()
            for plane in range(2):
                out_ref[plane, 0] += from_tiles[b - 1, plane * rows : (plane + 1) * rows, :].astype(F32)

    for b in (1, 2):

        @pl.when(tile + b < tile_count)
        def _():
            remote(to_tiles.at[b - 1], from_tiles.at[b - 1], 7 + b, partner).wait_send()


def shards(
    object_slices, probe_wave, propagator, tile_counts, row_offsets, column_offsets, intensity
):
    size = probe_wave.shape[1]
    rows, width = object_slices.shape[2:]
    mine = row_offsets.shape[0] // lax.axis_size("section")
    tile_count = lax.axis_size("tiles")
    smem = pl.BlockSpec(memory_space=pltpu.SMEM)
    vmem = pl.BlockSpec(memory_space=pltpu.VMEM)

    def body(*refs):
        kernel(tile_count, *refs)

    return pl.pallas_call(
        body,
        out_shape=jax.ShapeDtypeStruct(object_slices.shape, F32),
        in_specs=[smem, smem, smem, vmem, vmem, vmem, vmem, pl.BlockSpec(memory_space=pl.ANY)],
        out_specs=vmem,
        scratch_shapes=[
            pltpu.VMEM((2, 3, 2 * rows, width), BF16),
            pltpu.VMEM((2, mine, 3 * rows, 2 * size), BF16),
            pltpu.VMEM((width, mine * size), BF16),
            pltpu.VMEM((mine * size, width), BF16),
            pltpu.VMEM((mine, size, 3 * rows), BF16),
            pltpu.VMEM((mine, 3 * rows, size), BF16),
            pltpu.VMEM((2, 3, 2 * rows, width), F32),
            pltpu.VMEM((3, 2 * rows, width), BF16),
            pltpu.VMEM((3, 2 * rows, width), BF16),
            pltpu.VMEM((2, 2 * rows, width), BF16),
            pltpu.VMEM((2, 2 * rows, width), BF16),
            pltpu.VMEM((mine, size, size), F32),
            pltpu.SemaphoreType.DMA((10,)),
            pltpu.SemaphoreType.DMA((10,)),
            pltpu.SemaphoreType.DMA,
        ],
        compiler_params=pltpu.CompilerParams(
            collective_id=0, has_side_effects=True, vmem_limit_bytes=48 * 1024 * 1024
        ),
    )(
        tile_counts, row_offsets, column_offsets, object_slices, probe_wave, propagator,
        fourier_blocks(size), intensity,
    )


def solution(mesh):
    placed = (
        P(None, "section", ("groups", "tiles"), None),
        P(),
        P(),
        P(("groups", "tiles")),
        P(("groups", "tiles")),
        P(("groups", "tiles")),
        P(("groups", "tiles"), None, None),
    )
    return jax.shard_map(
        shards,
        mesh=mesh,
        in_specs=placed,
        out_specs=P(None, "section", ("groups", "tiles"), None),
        check_vma=False,
    )
```

time: 348 us -> 38.6 us (0.11)
  the two profiles are of different devices: /device:TPU:10 before, /device:TPU:18 now
where the time goes in v1:
time: 38.6 us; the launch traced here: 38.4 us
  Pallas kernels  31.9 us (83%)
  local copies, waits for them, and re-layouts  5.73 us (15%)
  between operations  0.72 us (2%)
    pallas_call x1, Pallas kernels, shards(): pl.pallas_call(body, out_shape=jax.ShapeDtypeStruct(object_slices.shape,...  31.9 us
    unnamed x15, local copies, waits for them, and re-layouts  5.73 us

profile of v1, /device:TPU:18, one launch (start us, length us, event | category | flops | bytes accessed | tf_op | source)
XLA Modules:
  0.0 38.4 jit_solution(13303740991680564121)
XLA Ops:
  0.0 0.0 copy-start.6
  0.0 0.0 copy-start.5
  0.7 0.0 copy-done.6
  0.7 0.0 copy-done.5
  0.7 0.0 copy-start
  0.7 1.1 %copy-done = f32[12,128,128]{2,1,0:T(8,128)S(1)} copy-done((f32[12,128,128]{2,1,0:T(8,128)S(1)}, f32[12,128,128]{2,1,0:T(8,128)}, u32[]{:S(2)}) %copy-start) | copy-done | bytes 786456
  1.8 0.0 copy-start.1
  1.8 1.0 %copy-done.1 = f32[2,1,64,1024]{3,2,1,0:T(8,128)S(1)} copy-done((f32[2,1,64,1024]{3,2,1,0:T(8,128)S(1)}, f32[2,1,64,1024]{3,2,1,0:T(8,128)}, u32[]{:S(2)}) %copy-start.1) | copy-done | bytes 524312
  2.9 0.0 copy-start.2
  2.9 0.9 %copy-done.2 = bf16[2,256,256]{2,1,0:T(8,128)(2,1)S(1)} copy-done((bf16[2,256,256]{2,1,0:T(8,128)(2,1)S(1)}, bf16[2,256,256]{2,1,0:T(8,128)(2,1)}, u32[]{:S(2)}) %copy-start.2) | copy-done | bytes 262168
  3.8 0.0 copy-start.3
  3.8 0.9 %copy-done.3 = f32[2,128,128]{2,1,0:T(8,128)S(1)} copy-done((f32[2,128,128]{2,1,0:T(8,128)S(1)}, f32[2,128,128]{2,1,0:T(8,128)}, u32[]{:S(2)}) %copy-start.3) | copy-done | bytes 131096
  4.7 0.0 copy-start.4
  4.7 0.9 %copy-done.4 = f32[2,128,128]{2,1,0:T(8,128)S(1)} copy-done((f32[2,128,128]{2,1,0:T(8,128)S(1)}, f32[2,128,128]{2,1,0:T(8,128)}, u32[]{:S(2)}) %copy-start.4) | copy-done | bytes 131096
  5.6 31.9 %shard_map.82 = f32[2,1,64,1024]{3,2,1,0:T(8,128)S(1)} custom-call(s32[1]{0:T(128)S(6)} %copy.10.refs_0_, s32[12]{0:T(128)S(1)} %copy-done.5, s32[12]{0:T(128)S(1)} %copy-done.6, f32[2,1,64,1024]{3,2,1,0:T(8,128)S(1)} %copy-done.1, f32[2,128,128]{2,1,0:T(8,128)S(1)} %copy-done.3, f32[2,128,128]{2,1,0:T(8,128)S(1)} %copy-done.4, ...), custom_call_target="tpu_custom_call" | custom-call | tf_op jit(solution)/shard_map/pallas_call | solution.py:265
  37.6 0.8 %copy.11 = f32[2,1,64,1024]{3,2,1,0:T(8,128)} copy(f32[2,1,64,1024]{3,2,1,0:T(8,128)S(1)} %shard_map.82) | data formatting | bytes 1048576
Async XLA Ops:
  0.0 0.7 %copy-start.6 = (s32[12]{0:T(128)S(1)}, s32[12]{0:T(128)}, u32[]{:S(2)}) copy-start(s32[12]{0:T(128)} %refs_2_.1) | copy-start | bytes 148
  0.0 0.7 %copy-start.5 = (s32[12]{0:T(128)S(1)}, s32[12]{0:T(128)}, u32[]{:S(2)}) copy-start(s32[12]{0:T(128)} %refs_1_.1) | copy-start | bytes 148
  0.7 1.1 %copy-start = (f32[12,128,128]{2,1,0:T(8,128)S(1)}, f32[12,128,128]{2,1,0:T(8,128)}, u32[]{:S(2)}) copy-start(f32[12,128,128]{2,1,0:T(8,128)} %refs_7_.1) | copy-start | bytes 2359300
  1.8 1.0 %copy-start.1 = (f32[2,1,64,1024]{3,2,1,0:T(8,128)S(1)}, f32[2,1,64,1024]{3,2,1,0:T(8,128)}, u32[]{:S(2)}) copy-start(f32[2,1,64,1024]{3,2,1,0:T(8,128)} %refs_3_.1) | copy-start | bytes 1572868
  2.9 0.9 %copy-start.2 = (bf16[2,256,256]{2,1,0:T(8,128)(2,1)S(1)}, bf16[2,256,256]{2,1,0:T(8,128)(2,1)}, u32[]{:S(2)}) copy-start(bf16[2,256,256]{2,1,0:T(8,128)(2,1)} %constant.2.clone.refs_6_) | copy-start | bytes 786436
  3.8 0.9 %copy-start.3 = (f32[2,128,128]{2,1,0:T(8,128)S(1)}, f32[2,128,128]{2,1,0:T(8,128)}, u32[]{:S(2)}) copy-start(f32[2,128,128]{2,1,0:T(8,128)} %refs_4_.1) | copy-start | bytes 393220
  4.7 0.9 %copy-start.4 = (f32[2,128,128]{2,1,0:T(8,128)S(1)}, f32[2,128,128]{2,1,0:T(8,128)}, u32[]{:S(2)}) copy-start(f32[2,128,128]{2,1,0:T(8,128)} %refs_5_.1) | copy-start | bytes 393220

commit v2 on v1

--- a/solution.py
+++ b/solution.py
@@ -10,6 +10,7 @@
 
 MESH = pl.DeviceIdType.MESH
 BF16 = jnp.bfloat16
+CHUNKS = 4
 F32 = jnp.float32
 
 
@@ -55,9 +56,10 @@
 
 
 def kernel(
-    tile_count, counts, row_offsets, column_offsets, object_ref, probe_ref, propagator_ref,
-    fourier_ref, intensity_hbm, out_ref, bands, strips, pick, place, pick_rows, place_rows, partial, to_partner,
-    from_partner, to_tiles, from_tiles, measured, send_sem, recv_sem, load_sem,
+    tile_count, counts_hbm, row_offsets_hbm, column_offsets_hbm, object_hbm, probe_hbm, propagator_hbm,
+    fourier_hbm, intensity_hbm, out_ref, counts, row_offsets, column_offsets, object_ref, probe_ref,
+    propagator_ref, fourier_ref, measured, bands, strips, pick, place, pick_rows, place_rows, partial,
+    to_partner, from_partner, to_next, to_mate, from_back, from_mate, relayed, send_sem, recv_sem, load_sem,
 ):
     size = probe_ref.shape[1]
     rows = object_ref.shape[2]
@@ -67,9 +69,28 @@
     core = lax.axis_index("section")
     other = 1 - core
     first = core * mine
-
-    load = pltpu.make_async_copy(intensity_hbm.at[pl.ds(first, mine)], measured, load_sem)
-    load.start()
+    odd = lax.rem(tile, 2) == 1
+    even = lax.rem(tile, 2) == 0
+    mate = tile + 1 - 2 * lax.rem(tile, 2)
+    has_mate = mate < tile_count
+
+    loads = [
+        pltpu.make_async_copy(source, held, load_sem.at[i])
+        for i, (source, held) in enumerate(
+            [
+                (object_hbm, object_ref),
+                (row_offsets_hbm, row_offsets),
+                (column_offsets_hbm, column_offsets),
+                (counts_hbm, counts),
+                (propagator_hbm, propagator_ref),
+                (fourier_hbm, fourier_ref),
+                (probe_hbm, probe_ref),
+                (intensity_hbm.at[pl.ds(first, mine)], measured),
+            ]
+        )
+    ]
+    for load in loads:
+        load.start()
 
     def remote(src, dst, index, where):
         return pltpu.make_async_remote_copy(
@@ -78,33 +99,51 @@
         )
 
     partner = {"section": other}
-
-    def towards(step):
-        return {"tiles": tile + step}
+    to_back = {"tiles": tile - 2}
+    to_ahead = {"tiles": tile + 2}
+    across = {"tiles": mate}
 
     barrier = pltpu.get_barrier_semaphore()
     pl.semaphore_signal(barrier, inc=1, device_id=partner, device_id_type=MESH)
     arrivals = jnp.int32(1)
-    for step in (-2, -1, 1, 2):
-        there = (tile + step >= 0) & (tile + step < tile_count)
+    for there, where in ((tile >= 2, to_back), (tile + 2 < tile_count, to_ahead), (has_mate, across)):
         arrivals = arrivals + there.astype(jnp.int32)
 
         @pl.when(there)
         def _():
-            pl.semaphore_signal(barrier, inc=1, device_id=towards(step), device_id_type=MESH)
-
+            pl.semaphore_signal(barrier, inc=1, device_id=where, device_id_type=MESH)
+
+    loads[0].wait()
     for plane in range(2):
         bands[core, 0, plane * rows : (plane + 1) * rows, :] = object_ref[plane, 0].astype(BF16)
     pl.semaphore_wait(barrier, arrivals)
 
-    own = remote(bands.at[core, 0], bands.at[core, 0], 0, partner)
-    for ahead in (1, 2):
-
-        @pl.when(tile >= ahead)
-        def _():
-            remote(bands.at[core, 0], bands.at[core, ahead], ahead, towards(-ahead)).start()
-
-    own.start()
+    piece = 2 * rows // CHUNKS
+
+    def part(c):
+        return pl.ds(c * piece, piece)
+
+    def chunk(layer, b, c):
+        return bands.at[layer, b, part(c)]
+
+    def band_copy(layer, source, target, c, kind, where):
+        return remote(chunk(layer, source, c), chunk(layer, target, c), CHUNKS * kind + c, where)
+
+    @pl.when(tile >= 2)
+    def _():
+        for c in range(CHUNKS):
+            band_copy(core, 0, 2, c, 2, to_back).start()
+
+    @pl.when(odd)
+    def _():
+        for c in range(CHUNKS):
+            band_copy(core, 0, 1, c, 1, across).start()
+
+    for c in range(CHUNKS):
+        band_copy(core, 0, 0, c, 0, partner).start()
+
+    for load in loads[1:7]:
+        load.wait()
 
     spots = lax.broadcasted_iota(jnp.int32, (size, width), 1)
     counter = lax.broadcasted_iota(jnp.int32, (size, width), 0)
@@ -147,32 +186,44 @@
                 bands[layer, ahead] = jnp.zeros((2 * rows, width), BF16)
 
     extract(core, 0)
-    own.wait()
+    for c in range(CHUNKS):
+        band_copy(core, 0, 0, c, 0, partner).wait()
     extract(other, 0)
-    for ahead in (1, 2):
-
-        @pl.when(tile + ahead < tile_count)
-        def _():
-            here = bands.at[core, ahead]
-            remote(here, here, ahead, partner).wait_recv()
-            remote(here, here, 2 + ahead, partner).start()
-
-        extract(core, ahead)
-
-    for ahead in (1, 2):
-
-        @pl.when(tile + ahead < tile_count)
-        def _():
-            here = bands.at[core, ahead]
-            there = bands.at[other, ahead]
-            remote(there, there, 2 + ahead, partner).wait_recv()
-            remote(here, here, 2 + ahead, partner).wait_send()
-
-        @pl.when(tile >= ahead)
-        def _():
-            remote(bands.at[core, 0], bands.at[core, ahead], ahead, towards(-ahead)).wait_send()
-
-        extract(other, ahead)
+
+    @pl.when(tile + 2 < tile_count)
+    def _():
+        for c in range(CHUNKS):
+            band_copy(core, 2, 2, c, 2, partner).wait_recv()
+
+            @pl.when(even)
+            def _():
+                band_copy(core, 2, 1, c, 1, across).start()
+
+            band_copy(core, 2, 2, c, 4, partner).start()
+
+    extract(core, 2)
+
+    @pl.when(tile + 1 < tile_count)
+    def _():
+        for c in range(CHUNKS):
+            band_copy(core, 1, 1, c, 1, partner).wait_recv()
+            band_copy(core, 1, 1, c, 3, partner).start()
+
+    extract(core, 1)
+
+    @pl.when(tile + 2 < tile_count)
+    def _():
+        for c in range(CHUNKS):
+            band_copy(other, 2, 2, c, 4, partner).wait_recv()
+
+    extract(other, 2)
+
+    @pl.when(tile + 1 < tile_count)
+    def _():
+        for c in range(CHUNKS):
+            band_copy(other, 1, 1, c, 3, partner).wait_recv()
+
+    extract(other, 1)
 
     patches = [[None] * mine for _ in range(2)]
     for layer in range(2):
@@ -186,7 +237,7 @@
     product = [cast(times(cast(middle[p], F32), patches[1][p]), BF16) for p in range(mine)]
     exit_waves = [cast(z, BF16) for z in sandwich(prop_turned, prop_plain, product)]
     far = sandwich(four_turned, four_plain, exit_waves)
-    load.wait()
+    loads[7].wait()
     misfit = []
     for p in range(mine):
         real, imag = far[p]
@@ -210,43 +261,121 @@
             ]
             partial[layer, b] = dot(jnp.concatenate(pieces, axis=0), place[...])
 
+    def swap(b):
+        return remote(to_partner.at[b], from_partner.at[b], 5 * CHUNKS + b, partner)
+
+    def piece_copy(source, target, c, kind, where):
+        return remote(source.at[part(c)], target.at[part(c)], CHUNKS * kind + c, where)
+
+    def give(layer):
+        @pl.when(core != layer)
+        def _():
+            for b in (1, 2, 0):
+                to_partner[b] = partial[layer, b].astype(BF16)
+                swap(b).start()
+
+    def hand_over(layer):
+        @pl.when(core == layer)
+        def _():
+            swap(1).wait_recv()
+            for c in range(CHUNKS):
+                to_mate[part(c)] = (partial[layer, 1, part(c)] + from_partner[1, part(c)].astype(F32)).astype(BF16)
+
+                @pl.when(even & has_mate)
+                def _():
+                    piece_copy(to_mate, from_mate, c, 6, across).start()
+
+                @pl.when(odd & (tile + 1 < tile_count))
+                def _():
+                    piece_copy(to_mate, relayed, c, 7, across).start()
+
+            swap(2).wait_recv()
+
+            @pl.when(tile + 2 < tile_count)
+            def _():
+                for c in range(CHUNKS):
+                    total = partial[layer, 2, part(c)] + from_partner[2, part(c)].astype(F32)
+
+                    @pl.when(odd)
+                    def _():
+                        to_next[part(c)] = total.astype(BF16)
+
+                    @pl.when(even)
+                    def _():
+                        piece_copy(to_mate, relayed, c, 7, across).wait_recv()
+                        to_next[part(c)] = (total + relayed[part(c)].astype(F32)).astype(BF16)
+
+                    piece_copy(to_next, from_back, c, 8, to_ahead).start()
+
     back = sandwich(prop_plain, prop_turned, adjoint)
     deposit(1, [conj_times(cast(middle[p], F32), back[p]) for p in range(mine)])
+    give(1)
     adjoint = [cast(conj_times(patches[1][p], back[p]), BF16) for p in range(mine)]
     back = sandwich(prop_plain, prop_turned, adjoint)
-    deposit(0, [conj_times(start, back[p]) for p in range(mine)])
-
-    swaps = []
-    for b in (1, 2, 0):
-        to_partner[b] = partial[other, b].astype(BF16)
-        swap = remote(to_partner.at[b], from_partner.at[b], 5 + b, partner)
-        swap.start()
-        swaps.append(swap)
-    for b, swap in zip((1, 2), swaps):
-        swap.wait()
-        to_tiles[b - 1] = (partial[core, b] + from_partner[b].astype(F32)).astype(BF16)
-
-        @pl.when(tile + b < tile_count)
-        def _():
-            remote(to_tiles.at[b - 1], from_tiles.at[b - 1], 7 + b, towards(b)).start()
-
-    swaps[2].wait()
+    gradients = [conj_times(start, back[p]) for p in range(mine)]
+    hand_over(1)
+    deposit(0, gradients)
+    give(0)
+    hand_over(0)
+
+    swap(0).wait_recv()
     total = partial[core, 0] + from_partner[0].astype(F32)
     for plane in range(2):
         out_ref[plane, 0] = total[plane * rows : (plane + 1) * rows]
-    for b in (1, 2):
-
-        @pl.when(tile >= b)
+
+    def add_in(received, kind):
+        for c in range(CHUNKS):
+            piece_copy(received, received, c, kind, across).wait_recv()
+            plane, inside = divmod(c * piece, rows)
+            out_ref[plane, 0, inside : inside + piece] += received[part(c)].astype(F32)
+
+    @pl.when(odd)
+    def _():
+        add_in(from_mate, 6)
+
+    @pl.when(tile >= 2)
+    def _():
+        add_in(from_back, 8)
+
+    @pl.when(tile >= 2)
+    def _():
+        for c in range(CHUNKS):
+            band_copy(core, 0, 2, c, 2, partner).wait_send()
+
+    @pl.when(odd)
+    def _():
+        for c in range(CHUNKS):
+            band_copy(core, 0, 1, c, 1, partner).wait_send()
+
+    @pl.when(tile + 2 < tile_count)
+    def _():
+        @pl.when(even)
         def _():
-            remote(to_tiles.at[b - 1], from_tiles.at[b - 1], 7 + b, partner).wait_recv()
-            for plane in range(2):
-                out_ref[plane, 0] += from_tiles[b - 1, plane * rows : (plane + 1) * rows, :].astype(F32)
-
-    for b in (1, 2):
-
-        @pl.when(tile + b < tile_count)
-        def _():
-            remote(to_tiles.at[b - 1], from_tiles.at[b - 1], 7 + b, partner).wait_send()
+            for c in range(CHUNKS):
+                band_copy(core, 2, 1, c, 1, partner).wait_send()
+
+        for c in range(CHUNKS):
+            band_copy(core, 2, 2, c, 4, partner).wait_send()
+        for c in range(CHUNKS):
+            piece_copy(to_next, from_back, c, 8, partner).wait_send()
+
+    @pl.when(tile + 1 < tile_count)
+    def _():
+        for c in range(CHUNKS):
+            band_copy(core, 1, 1, c, 3, partner).wait_send()
+
+    for b in range(3):
+        swap(b).wait_send()
+
+    @pl.when(even & has_mate)
+    def _():
+        for c in range(CHUNKS):
+            piece_copy(to_mate, from_mate, c, 6, partner).wait_send()
+
+    @pl.when(odd & (tile + 1 < tile_count))
+    def _():
+        for c in range(CHUNKS):
+            piece_copy(to_mate, relayed, c, 7, partner).wait_send()
 
 
 def shards(
@@ -256,8 +385,9 @@
     rows, width = object_slices.shape[2:]
     mine = row_offsets.shape[0] // lax.axis_size("section")
     tile_count = lax.axis_size("tiles")
-    smem = pl.BlockSpec(memory_space=pltpu.SMEM)
+    anywhere = pl.BlockSpec(memory_space=pl.ANY)
     vmem = pl.BlockSpec(memory_space=pltpu.VMEM)
+    band = pltpu.VMEM((2 * rows, width), BF16)
 
     def body(*refs):
         kernel(tile_count, *refs)
@@ -265,9 +395,17 @@
     return pl.pallas_call(
         body,
         out_shape=jax.ShapeDtypeStruct(object_slices.shape, F32),
-        in_specs=[smem, smem, smem, vmem, vmem, vmem, vmem, pl.BlockSpec(memory_space=pl.ANY)],
+        in_specs=[anywhere] * 8,
         out_specs=vmem,
         scratch_shapes=[
+            pltpu.SMEM(tile_counts.shape, jnp.int32),
+            pltpu.SMEM(row_offsets.shape, jnp.int32),
+            pltpu.SMEM(column_offsets.shape, jnp.int32),
+            pltpu.VMEM(object_slices.shape, F32),
+            pltpu.VMEM(probe_wave.shape, F32),
+            pltpu.VMEM(propagator.shape, F32),
+            pltpu.VMEM((2, 2 * size, 2 * size), BF16),
+            pltpu.VMEM((mine, size, size), F32),
             pltpu.VMEM((2, 3, 2 * rows, width), BF16),
             pltpu.VMEM((2, mine, 3 * rows, 2 * size), BF16),
             pltpu.VMEM((width, mine * size), BF16),
@@ -277,15 +415,17 @@
             pltpu.VMEM((2, 3, 2 * rows, width), F32),
             pltpu.VMEM((3, 2 * rows, width), BF16),
             pltpu.VMEM((3, 2 * rows, width), BF16),
-            pltpu.VMEM((2, 2 * rows, width), BF16),
-            pltpu.VMEM((2, 2 * rows, width), BF16),
-            pltpu.VMEM((mine, size, size), F32),
-            pltpu.SemaphoreType.DMA((10,)),
-            pltpu.SemaphoreType.DMA((10,)),
-            pltpu.SemaphoreType.DMA,
+            band,
+            band,
+            band,
+            band,
+            band,
+            pltpu.SemaphoreType.DMA((9 * CHUNKS,)),
+            pltpu.SemaphoreType.DMA((9 * CHUNKS,)),
+            pltpu.SemaphoreType.DMA((8,)),
         ],
         compiler_params=pltpu.CompilerParams(
-            collective_id=0, has_side_effects=True, vmem_limit_bytes=48 * 1024 * 1024
+            collective_id=0, has_side_effects=True, vmem_limit_bytes=60 * 1024 * 1024
         ),
     )(
         tile_counts, row_offsets, column_offsets, object_slices, probe_wave, propagator,

time: 38.6 us -> 35.3 us (0.915)
  the two profiles are of different devices: /device:TPU:18 before, /device:TPU:0 now
where the time goes in v2:
time: 35.3 us; the launch traced here: 35.2 us
  Pallas kernels  32.6 us (92%)
  local copies, waits for them, and re-layouts  1.89 us (5%)
  between operations  0.66 us (2%)
    pallas_call x1, Pallas kernels, shards(): pl.pallas_call(body, out_shape=jax.ShapeDtypeStruct(object_slices.shape,...  32.6 us
    unnamed x1, local copies, waits for them, and re-layouts  1.89 us

profile of v2, /device:TPU:0, one launch (start us, length us, event | category | flops | bytes accessed | tf_op | source)
XLA Modules:
  0.0 35.2 jit_solution(4820702295971180608)
XLA Ops:
  0.7 32.6 %shard_map.82 = f32[2,1,64,1024]{3,2,1,0:T(8,128)} custom-call(s32[1]{0:T(128)S(6)} %copy.10.refs_0_, s32[12]{0:T(128)} %refs_1_.1, s32[12]{0:T(128)} %refs_2_.1, f32[2,1,64,1024]{3,2,1,0:T(8,128)} %refs_3_.1, f32[2,128,128]{2,1,0:T(8,128)} %refs_4_.1, f32[2,128,128]{2,1,0:T(8,128)} %refs_5_.1, bf16[2,256,256]{2,1,0:T(8,128)(2,1)} %constant.2.clone.refs_6_, ...), custom_call_target="tpu_custom_call" | custom-call | tf_op jit(solution)/shard_map/pallas_call | solution.py:395
  33.3 1.9 %copy.11 = f32[2,1,64,1024]{3,2,1,0:T(8,128)} copy(f32[2,1,64,1024]{3,2,1,0:T(8,128)} %shard_map.82) | data formatting | bytes 1048576

commit v3 on v2

--- a/solution.py
+++ b/solution.py
@@ -10,7 +10,7 @@
 
 MESH = pl.DeviceIdType.MESH
 BF16 = jnp.bfloat16
-CHUNKS = 4
+CHUNKS = 8
 F32 = jnp.float32
 
 

time: 35.3 us -> 35.3 us (level)
  no operation moved by 1% of the time
where the time goes in v3:
time: 35.3 us; the launch traced here: 35.1 us
  Pallas kernels  32.5 us (92%)
  local copies, waits for them, and re-layouts  1.89 us (5%)
  between operations  0.66 us (2%)
    pallas_call x1, Pallas kernels, shards(): pl.pallas_call(body, out_shape=jax.ShapeDtypeStruct(object_slices.shape,...  32.5 us
    unnamed x1, local copies, waits for them, and re-layouts  1.89 us

profile of v3, /device:TPU:0, one launch (start us, length us, event | category | flops | bytes accessed | tf_op | source)
XLA Modules:
  0.0 35.1 jit_solution(10992297825682444914)
XLA Ops:
  0.7 32.5 %shard_map.82 = f32[2,1,64,1024]{3,2,1,0:T(8,128)} custom-call(s32[1]{0:T(128)S(6)} %copy.10.refs_0_, s32[12]{0:T(128)} %refs_1_.1, s32[12]{0:T(128)} %refs_2_.1, f32[2,1,64,1024]{3,2,1,0:T(8,128)} %refs_3_.1, f32[2,128,128]{2,1,0:T(8,128)} %refs_4_.1, f32[2,128,128]{2,1,0:T(8,128)} %refs_5_.1, bf16[2,256,256]{2,1,0:T(8,128)(2,1)} %constant.2.clone.refs_6_, ...), custom_call_target="tpu_custom_call" | custom-call | tf_op jit(solution)/shard_map/pallas_call | solution.py:395
  33.2 1.9 %copy.11 = f32[2,1,64,1024]{3,2,1,0:T(8,128)} copy(f32[2,1,64,1024]{3,2,1,0:T(8,128)} %shard_map.82) | data formatting | bytes 1048576

commit v4 on v3

--- a/solution.py
+++ b/solution.py
@@ -291,21 +291,21 @@
 
             swap(2).wait_recv()
 
-            @pl.when(tile + 2 < tile_count)
+            @pl.when(odd & (tile + 2 < tile_count))
             def _():
                 for c in range(CHUNKS):
                     total = partial[layer, 2, part(c)] + from_partner[2, part(c)].astype(F32)
-
-                    @pl.when(odd)
-                    def _():
-                        to_next[part(c)] = total.astype(BF16)
-
-                    @pl.when(even)
-                    def _():
-                        piece_copy(to_mate, relayed, c, 7, across).wait_recv()
-                        to_next[part(c)] = (total + relayed[part(c)].astype(F32)).astype(BF16)
-
+                    to_next[part(c)] = total.astype(BF16)
                     piece_copy(to_next, from_back, c, 8, to_ahead).start()
+
+    def send_relayed(layer):
+        @pl.when((core == layer) & even & (tile + 2 < tile_count))
+        def _():
+            for c in range(CHUNKS):
+                total = partial[layer, 2, part(c)] + from_partner[2, part(c)].astype(F32)
+                piece_copy(to_mate, relayed, c, 7, across).wait_recv()
+                to_next[part(c)] = (total + relayed[part(c)].astype(F32)).astype(BF16)
+                piece_copy(to_next, from_back, c, 8, to_ahead).start()
 
     back = sandwich(prop_plain, prop_turned, adjoint)
     deposit(1, [conj_times(cast(middle[p], F32), back[p]) for p in range(mine)])
@@ -316,7 +316,9 @@
     hand_over(1)
     deposit(0, gradients)
     give(0)
+    send_relayed(1)
     hand_over(0)
+    send_relayed(0)
 
     swap(0).wait_recv()
     total = partial[core, 0] + from_partner[0].astype(F32)

time: 35.3 us -> 33.9 us (0.960)
  Pallas kernels: 32.5 us -> 31.2 us
    pallas_call x1, Pallas kernels: 32.5 us -> 31.2 us  [shards(): pl.pallas_call(body, out_shape=jax.ShapeDtypeStruct(object_slices.shape,...]
where the time goes in v4:
time: 33.9 us; the launch traced here: 33.7 us
  Pallas kernels  31.2 us (92%)
  local copies, waits for them, and re-layouts  1.89 us (6%)
  between operations  0.66 us (2%)
    pallas_call x1, Pallas kernels, shards(): pl.pallas_call(body, out_shape=jax.ShapeDtypeStruct(object_slices.shape,...  31.2 us
    unnamed x1, local copies, waits for them, and re-layouts  1.89 us

profile of v4, /device:TPU:0, one launch (start us, length us, event | category | flops | bytes accessed | tf_op | source)
XLA Modules:
  0.0 33.7 jit_solution(14388349213591532282)
XLA Ops:
  0.7 31.2 %shard_map.82 = f32[2,1,64,1024]{3,2,1,0:T(8,128)} custom-call(s32[1]{0:T(128)S(6)} %copy.10.refs_0_, s32[12]{0:T(128)} %refs_1_.1, s32[12]{0:T(128)} %refs_2_.1, f32[2,1,64,1024]{3,2,1,0:T(8,128)} %refs_3_.1, f32[2,128,128]{2,1,0:T(8,128)} %refs_4_.1, f32[2,128,128]{2,1,0:T(8,128)} %refs_5_.1, bf16[2,256,256]{2,1,0:T(8,128)(2,1)} %constant.2.clone.refs_6_, ...), custom_call_target="tpu_custom_call" | custom-call | tf_op jit(solution)/shard_map/pallas_call | solution.py:397
  31.8 1.9 %copy.11 = f32[2,1,64,1024]{3,2,1,0:T(8,128)} copy(f32[2,1,64,1024]{3,2,1,0:T(8,128)} %shard_map.82) | data formatting | bytes 1048576
